TPU v7x, 256 devices: a whole 4x4x8 slice. The times are simulated.
256 devices in a mesh: tm: 16 (over y, x_lo, core), space: 16 (over z, x_hi).
Axes of the slice: x: 4 (x_hi: 2, x_lo: 2; x = x_hi * 2 + x_lo), y: 4, z: 8, core: 2. Of those that a mesh axis runs over, the one named last changes fastest.
Arguments:
- video: bfloat16 [256, 64, 2048], P('space', 'tm'), may hold values from -120 to 120
- frame_ids: int32 [64], P('tm'), may hold values from 0 to 63, as said below
- gains: float32 [3, 2048], replicated, may hold values from 0.1 to 1.9
- spatial_qkv: bfloat16 [3, 2048, 2048], P(None, None, 'space'), may hold values from -2 to 2
- spatial_out: bfloat16 [2048, 2048], P('space'), may hold values from -0.75 to 0.75
- temporal_qkv: bfloat16 [3, 2048, 2048], P(None, None, 'space'), may hold values from -2 to 2
- temporal_out: bfloat16 [2048, 2048], P('space'), may hold values from -0.125 to 0.125
- mlp_in: bfloat16 [2048, 8192], P(None, 'space'), may hold values from -0.125 to 0.125
- mlp_out: bfloat16 [8192, 2048], P('space'), may hold values from -0.0625 to 0.0625
Outputs:
- block_out: bfloat16 [256, 64, 2048], P('space', 'tm')
Inputs may be any that keep to these rules, and one draw needn't show every extreme that they name: `frame_ids`: a permutation of 0 to 63 in which frame slots 2j and 2j + 1 hold frames k and 63 - k for some k.
All inputs are finite; a program needn't handle non-finite values.
Results may differ from a plain program's by a relative error of at most 0.02.
Values may be sent and summed in bfloat16 or wider, within the bound.
No kernel may reach another device: no remote copies, remote signals or barrier semaphores. Data moves between devices by JAX's collectives and lax.ppermute only.
A program may use at most 128 MiB of HBM per device.

v0:
```python
import math

import jax
import jax.numpy as jnp
from jax import lax
from jax.sharding import PartitionSpec as P

HEAD_DIM = 128


def normed(value, gain):
    meansq = jnp.mean(value * value, axis=-1, keepdims=True)
    return value * lax.rsqrt(meansq + 1e-06) * gain


def project(piece, weight):
    return jnp.einsum("rfd,cde->rfce", piece, weight, preferred_element_type=jnp.float32).astype(
        jnp.bfloat16
    )


def spatial_attend(packed):
    tokens, frames, _, width = packed.shape
    local_heads = width // HEAD_DIM
    query = packed[:, :, 0].reshape(tokens, frames, local_heads, HEAD_DIM)
    keys = packed[:, :, 1].reshape(tokens, frames, local_heads, HEAD_DIM)
    values = packed[:, :, 2].reshape(tokens, frames, local_heads, HEAD_DIM)
    scores = jnp.einsum(
        "pfhe,qfhe->fhpq", query, keys, preferred_element_type=jnp.float32
    ) / math.sqrt(HEAD_DIM)
    weights = jax.nn.softmax(scores, axis=-1).astype(jnp.bfloat16)
    result = jnp.einsum("fhpq,qfhe->pfhe", weights, values, preferred_element_type=jnp.float32)
    return result.astype(jnp.bfloat16).reshape(tokens, frames, width)


def temporal_attend(packed, frame_ids):
    tokens, frames, _, width = packed.shape
    local_heads = width // HEAD_DIM
    query = packed[:, :, 0].reshape(tokens, frames, local_heads, HEAD_DIM)
    pairs = packed[:, :, 1:]
    stamps = frame_ids.reshape(1, frames)
    start_max = jnp.full((tokens, local_heads, frames), -1e30, jnp.float32)
    run_max = start_max
    kv_piece = lax.all_gather(pairs, "tm", axis=1, tiled=True)
    id_piece = lax.all_gather(stamps, "tm", axis=1, tiled=True)
    count = kv_piece.shape[1]
    keys = kv_piece[:, :, 0].reshape(tokens, count, local_heads, HEAD_DIM)
    values = kv_piece[:, :, 1].reshape(tokens, count, local_heads, HEAD_DIM).astype(jnp.float32)
    scores = jnp.einsum(
        "pfhe,pghe->phfg", query, keys, preferred_element_type=jnp.float32
    ) / math.sqrt(HEAD_DIM)
    visible = id_piece[0][None, None, None, :] <= frame_ids[None, None, :, None]
    scores = jnp.where(visible, scores, -1e30)
    new_max = jnp.maximum(run_max, jnp.max(scores, axis=-1))
    probs = jnp.exp(scores - new_max[..., None])
    run_sum = jnp.sum(probs, axis=-1)
    update = jnp.einsum("phfg,pghe->phfe", probs, values, precision=lax.Precision.HIGHEST)
    accum = update
    run_max, run_sum, accum = (new_max, run_sum, accum)
    result = accum / run_sum[..., None]
    return jnp.transpose(result, (0, 2, 1, 3)).astype(jnp.bfloat16).reshape(tokens, frames, width)


def body(
    video, frame_ids, gains, spatial_qkv, spatial_out, temporal_qkv, temporal_out, mlp_in, mlp_out
):
    state = video.astype(jnp.float32)
    first = normed(state, gains[0]).astype(jnp.bfloat16)
    packed = project(lax.all_gather(first, "space", axis=0, tiled=True), spatial_qkv)
    spatial = spatial_attend(packed)
    rows = spatial
    second_state = state + lax.psum_scatter(
        jnp.einsum("pfd,de->pfe", rows, spatial_out, preferred_element_type=jnp.float32).astype(
            jnp.bfloat16
        ),
        "space",
        scatter_dimension=0,
        tiled=True,
    ).astype(jnp.float32)
    second = normed(second_state, gains[1]).astype(jnp.bfloat16)
    tpacked = project(lax.all_gather(second, "space", axis=0, tiled=True), temporal_qkv)
    temporal = temporal_attend(tpacked, frame_ids)
    rows = temporal
    own_state = second_state + lax.psum_scatter(
        jnp.einsum("pfd,de->pfe", rows, temporal_out, preferred_element_type=jnp.float32).astype(
            jnp.bfloat16
        ),
        "space",
        scatter_dimension=0,
        tiled=True,
    ).astype(jnp.float32)
    third = normed(own_state, gains[2]).astype(jnp.bfloat16)
    inner = jnp.einsum(
        "rfd,dk->rfk",
        lax.all_gather(third, "space", axis=0, tiled=True),
        mlp_in,
        preferred_element_type=jnp.float32,
    )
    hidden = jax.nn.gelu(inner, approximate=True).astype(jnp.bfloat16)
    rows = hidden
    result = own_state + lax.psum_scatter(
        jnp.einsum("pfk,kd->pfd", rows, mlp_out, preferred_element_type=jnp.float32).astype(
            jnp.bfloat16
        ),
        "space",
        scatter_dimension=0,
        tiled=True,
    ).astype(jnp.float32)
    return result.astype(jnp.bfloat16)


def solution(mesh):
    return jax.shard_map(
        body,
        mesh=mesh,
        in_specs=(
            P("space", "tm", None),
            P("tm"),
            P(),
            P(None, None, "space"),
            P("space", None),
            P(None, None, "space"),
            P("space", None),
            P(None, "space"),
            P("space", None),
        ),
        out_specs=P("space", "tm", None),
        check_vma=False,
    )
```

profile of v0, /device:TPU:8, one launch (start us, length us, event | category | flops | bytes accessed | tf_op | source)
XLA Modules:
  0.0 1055.2 jit_solution(12636430041494405385)
XLA Ops:
  6.5 0.0 copy-start
  6.5 0.0 all-gather.6.cloned.1.call-start
  6.5 1.4 fusion.40
  7.9 0.9 fusion.61
  8.8 1.8 fusion.42
  10.7 0.0 all-gather.6.cloned.1.call-update
  10.7 0.0 reduce-scatter.4.cloned.1.call-start
  10.7 103.0 %all-gather.6.cloned.1.call-done = bf16[256,4,2048]{2,0,1:T(8,128)(2,1)} async-done(((bf16[16,4,2048]{2,0,1:T(8,128)(2,1)}), bf16[256,4,2048]{2,0,1:T(8,128)(2,1)}) %all-gather.6.cloned.1.call-update) | async-done | bytes 4194320 | tf_op jit(solution)/shard_map/all_gather | solution.py:69
  113.8 5.0 fusion.22
  118.8 0.0 copy-start.5
  118.8 0.9 copy-done.5
  119.7 0.5 fusion.62
  120.1 1.3 convolution_multiply_fusion
  121.5 0.0 copy-start.1
  121.5 4.7 convolution_convert_fusion.2
  126.2 0.0 reduce-scatter.4.cloned.1.call-update
  126.3 0.0 all-gather.8.cloned.1.call-start
  126.3 209.0 %reduce-scatter.4.cloned.1.call-done = bf16[16,4,2048]{2,0,1:T(8,128)(2,1)} async-done(((bf16[256,4,2048]{2,0,1:T(8,128)(2,1)}), bf16[16,4,2048]{2,0,1:T(8,128)(2,1)}) %reduce-scatter.4.cloned.1.call-update) | async-done | bytes 262160 | tf_op jit(solution)/shard_map/reduce_scatter | solution.py:72
  335.3 0.0 copy-done.1
  335.3 1.2 multiply_reduce_fusion.1
  336.5 1.9 multiply_convert_fusion.1
  338.4 0.0 all-gather.8.cloned.1.call-update
  338.4 0.0 copy-start.7
  338.4 0.0 copy-start.6
  338.4 0.0 all-gather.10.cloned.1.call-start
  338.5 98.2 %all-gather.8.cloned.1.call-done = bf16[256,4,2048]{2,0,1:T(8,128)(2,1)} async-done(((bf16[16,4,2048]{2,0,1:T(8,128)(2,1)}), bf16[256,4,2048]{2,0,1:T(8,128)(2,1)}) %all-gather.8.cloned.1.call-update) | async-done | bytes 4194320 | tf_op jit(solution)/shard_map/all_gather | solution.py:81
  436.7 5.0 fusion.27
  441.7 0.9 slice.44
  442.6 0.0 all-gather.10.cloned.1.call-update
  442.6 0.0 reduce-scatter.6.cloned.1.call-start
  442.7 0.0 copy-done.7
  442.7 0.6 dynamic-slice
  443.9 0.0 copy-done.6
  443.9 0.2 dynamic-update-slice
  444.2 10.5 all-reduce
  454.7 0.1 broadcast_compare_fusion
  454.8 39.3 %all-gather.10.cloned.1.call-done = bf16[256,64,2,128]{3,0,2,1:T(8,128)(2,1)} async-done(((bf16[256,4,2,128]{3,0,2,1:T(8,128)(2,1)}), bf16[256,64,2,128]{3,0,2,1:T(8,128)(2,1)}) %all-gather.10.cloned.1.call-update) | async-done | bytes 8388624 | tf_op jit(solution)/shard_map/all_gather | solution.py:44
  494.0 4.0 fusion.60
  498.0 3.1 fusion.63
  501.1 0.0 copy-start.4
  501.1 0.7 fusion.48
  501.9 6.9 fusion.6
  508.7 0.1 copy.23
  508.8 0.0 copy-done.4
  508.8 0.0 copy-start.2
  508.8 4.3 convolution_convert_fusion.1
  513.1 0.0 reduce-scatter.6.cloned.1.call-update
  513.2 0.0 all-gather.12.cloned.1.call-start
  513.2 213.1 %reduce-scatter.6.cloned.1.call-done = bf16[16,4,2048]{2,0,1:T(8,128)(2,1)} async-done(((bf16[256,4,2048]{2,0,1:T(8,128)(2,1)}), bf16[16,4,2048]{2,0,1:T(8,128)(2,1)}) %reduce-scatter.6.cloned.1.call-update) | async-done | bytes 262160 | tf_op jit(solution)/shard_map/reduce_scatter | solution.py:84
  726.3 0.0 copy-done.2
  726.3 1.2 multiply_reduce_fusion
  727.6 1.9 multiply_convert_fusion
  729.5 0.0 all-gather.12.cloned.1.call-update
  729.5 0.3 reduce-scatter.8.cloned.1.call-start
  729.8 98.0 %all-gather.12.cloned.1.call-done = bf16[256,4,2048]{2,0,1:T(8,128)(2,1)} async-done(((bf16[16,4,2048]{2,0,1:T(8,128)(2,1)}), bf16[256,4,2048]{2,0,1:T(8,128)(2,1)}) %all-gather.12.cloned.1.call-update) | async-done | bytes 4194320 | tf_op jit(solution)/shard_map/all_gather | solution.py:95
  827.7 0.0 copy-done
  827.7 9.6 convolution_convert_fusion
  837.3 0.0 copy-start.3
  837.3 0.0 reduce-scatter.8.cloned.1.call-update
  837.3 208.9 %reduce-scatter.8.cloned.1.call-done = bf16[16,4,2048]{2,0,1:T(8,128)(2,1)} async-done(((bf16[256,4,2048]{2,0,1:T(8,128)(2,1)}), bf16[16,4,2048]{2,0,1:T(8,128)(2,1)}) %reduce-scatter.8.cloned.1.call-update) | async-done | bytes 262160 | tf_op jit(solution)/shard_map/reduce_scatter | solution.py:101
  1046.2 0.0 copy-done.3
  1046.2 1.2 add_convert_fusion
  1047.4 0.9 copy.24
  (6 shorter events, 0.1 us)
Async XLA Ops:
  6.5 821.2 %copy-start = (bf16[512,2048]{1,0:T(8,128)(2,1)S(1)}, bf16[512,2048]{1,0:T(8,128)(2,1)}, u32[]{:S(2)}) copy-start(bf16[512,2048]{1,0:T(8,128)(2,1)} %param.17) | copy-start | bytes 6291460
  6.5 107.2 %all-gather.6.cloned.1.call-start = ((), (), s32[]{:S(2)}) async-start(), calls=%async_computation.3 | async-start | bytes 4456448 | tf_op jit(solution)/shard_map/all_gather | solution.py:69
  10.7 324.6 %reduce-scatter.4.cloned.1.call-start = ((), (), s32[]{:S(2)}) async-start(), calls=%async_computation.4 | async-start | bytes 4456448 | tf_op jit(solution)/shard_map/reduce_scatter | solution.py:72
  118.8 0.9 copy-start.5
  121.5 213.8 %copy-start.1 = (bf16[16,4,2048]{2,1,0:T(4,128)(2,1)S(1)}, bf16[16,4,2048]{2,1,0:T(4,128)(2,1)}, u32[]{:S(2)}) copy-start(bf16[16,4,2048]{2,1,0:T(4,128)(2,1)} %param.9) | copy-start | bytes 786436
  126.3 310.4 %all-gather.8.cloned.1.call-start = ((), (), s32[]{:S(2)}) async-start(), calls=%async_computation.5 | async-start | bytes 4456448 | tf_op jit(solution)/shard_map/all_gather | solution.py:81
  338.4 104.3 %copy-start.7 = (u32[256]{0:T(256)S(1)}, u32[256]{0:T(256)}, u32[]{:S(2)}) copy-start(u32[256]{0:T(256)} %constant.32) | copy-start | bytes 3076
  338.4 105.5 %copy-start.6 = (s32[4]{0:T(128)S(1)}, s32[4]{0:T(128)}, u32[]{:S(2)}) copy-start(s32[4]{0:T(128)} %param.10) | copy-start | bytes 52
  338.4 155.6 %all-gather.10.cloned.1.call-start = ((), (), s32[]{:S(2)}) async-start(), calls=%async_computation.6 | async-start | bytes 8912896 | tf_op jit(solution)/shard_map/all_gather | solution.py:44
  442.6 283.7 %reduce-scatter.6.cloned.1.call-start = ((), (), s32[]{:S(2)}) async-start(), calls=%async_computation.7 | async-start | bytes 4456448 | tf_op jit(solution)/shard_map/reduce_scatter | solution.py:84
  501.1 7.7 copy-start.4
  508.8 217.5 %copy-start.2 = (bf16[16,4,2048]{2,0,1:T(8,128)(2,1)S(1)}, bf16[16,4,2048]{2,0,1:T(8,128)(2,1)}, u32[]{:S(2)}) copy-start(bf16[16,4,2048]{2,0,1:T(8,128)(2,1)} %reduce-scatter.4.cloned.1.call-done) | copy-start | bytes 786436
  513.2 314.6 %all-gather.12.cloned.1.call-start = ((), (), s32[]{:S(2)}) async-start(), calls=%async_computation.8 | async-start | bytes 4456448 | tf_op jit(solution)/shard_map/all_gather | solution.py:95
  729.5 316.8 %reduce-scatter.8.cloned.1.call-start = ((), (), s32[]{:S(2)}) async-start(), calls=%async_computation.9 | async-start | bytes 4456448 | tf_op jit(solution)/shard_map/reduce_scatter | solution.py:101
  837.3 208.9 %copy-start.3 = (bf16[16,4,2048]{2,0,1:T(8,128)(2,1)S(1)}, bf16[16,4,2048]{2,0,1:T(8,128)(2,1)}, u32[]{:S(2)}) copy-start(bf16[16,4,2048]{2,0,1:T(8,128)(2,1)} %reduce-scatter.6.cloned.1.call-done) | copy-start | bytes 786436
Sparse Core Ops, SparseCore 0:
  10.8 102.9 all-gather.5
  126.4 208.8 reduce-scatter.3
  338.5 98.1 all-gather.7
  442.7 51.2 all-gather.9
  513.3 212.9 reduce-scatter.5
  729.6 98.0 all-gather.11
  837.5 208.7 reduce-scatter.7
where the time goes:
time: 1060 us
  waiting for transfers between devices  970 us (92%)
  matrix products  40.4 us (4%)
  between operations  14.3 us (1%)
  other arithmetic  11.4 us (1%)
    reduce_scatter x1, waiting for transfers between devices, body(): lax.psum_scatter(jnp.einsum('pfd,de->pfe', rows, temporal_out, preferred_...  213 us
    reduce_scatter x1, waiting for transfers between devices, body(): lax.psum_scatter(jnp.einsum('pfd,de->pfe', rows, spatial_out, preferred_e...  209 us
    reduce_scatter x1, waiting for transfers between devices, body(): lax.psum_scatter(jnp.einsum('pfk,kd->pfd', rows, mlp_out, preferred_eleme...  209 us
    all_gather x1, waiting for transfers between devices, body(): lax.all_gather(first, 'space', axis=0, tiled=True)  103 us
    all_gather x1, waiting for transfers between devices, body(): lax.all_gather(second, 'space', axis=0, tiled=True)  98.2 us
    all_gather x1, waiting for transfers between devices, body(): lax.all_gather(third, 'space', axis=0, tiled=True)  98 us
    all_gather x1, waiting for transfers between devices, temporal_attend(): kv_piece = lax.all_gather(pairs, 'tm', axis=1, tiled=True)  39.3 us
  transfers between devices with their start and end apart: 7, of which 7 were waited for; matrix products, arithmetic and copies ran while one was open for 0% of the time, Pallas kernels for 0%

commit v1 on v0

v1 whole, which is shorter than its diff:
```python
import math

import jax
import jax.numpy as jnp
from jax import lax
from jax.experimental import pallas as pl
from jax.experimental.pallas import tpu as pltpu
from jax.sharding import Mesh, PartitionSpec as P

HEAD_DIM = 128
SCALE = 1.0 / math.sqrt(HEAD_DIM)
F32 = jnp.float32
BF16 = jnp.bfloat16
TM = ("y", "xl", "c")
PEERS = ("y", "xl", "c", "xh")
SWAP = [(0, 1), (1, 0)]
MIB = 1 << 20


def normed(value, gain):
    meansq = jnp.mean(value * value, axis=-1, keepdims=True)
    return value * lax.rsqrt(meansq + 1e-06) * gain


def dot(a, b):
    return jnp.dot(a, b, preferred_element_type=F32)


def dot_t(a, b):
    return lax.dot_general(a, b, (((1,), (1,)), ((), ())), preferred_element_type=F32)


def ring_gather(block, tied=None):
    size = 8
    right = [(i, (i + 1) % size) for i in range(size)]
    left = [(i, (i - 1) % size) for i in range(size)]
    z = lax.axis_index("z")
    rows = block.shape[0]
    out = jnp.zeros((size,) + block.shape, block.dtype)
    put = lambda out, part, owner, row: lax.dynamic_update_slice(
        out, part[None], (lax.rem(owner + 2 * size, size), row, 0)
    )
    out = put(out, block, z, 0)
    fwd = bwd = block
    for step in range(1, 4):
        fwd = lax.ppermute(fwd, "z", right)
        bwd = lax.ppermute(bwd, "z", left)
        out = put(out, fwd, z - step, 0)
        out = put(out, bwd, z + step, 0)
    if tied is not None:
        fwd, bwd, tied = lax.optimization_barrier((fwd, bwd, tied))
    half = rows // 2
    fwd = lax.ppermute(fwd[:half], "z", right)
    bwd = lax.ppermute(bwd[half:], "z", left)
    out = put(out, fwd, z - 4, 0)
    out = put(out, bwd, z + 4, half)
    return out, tied


def spatial_kernel(first_ref, h_ref, own_ref, other_ref, out_ref):
    rows = h_ref.shape[0]
    frame_q = (lax.broadcasted_iota(jnp.int32, (rows, rows), 0) // 8) % 2
    frame_k = (lax.broadcasted_iota(jnp.int32, (rows, rows), 1) // 8) % 2
    same = frame_q == frame_k
    hidden = h_ref[...]

    def head(w_ref):
        query = dot(hidden, w_ref[0]).astype(BF16)
        keys = dot(hidden, w_ref[1]).astype(BF16)
        values = dot(hidden, w_ref[2]).astype(BF16)
        scores = jnp.where(same, dot_t(query, keys) * SCALE, -1e30)
        top = jnp.max(scores, axis=-1, keepdims=True)
        probs = jnp.exp(scores - top)
        total = jnp.sum(probs, axis=-1, keepdims=True)
        weights = (probs / total).astype(BF16)
        return dot(weights, values).astype(BF16)

    mine, other = head(own_ref), head(other_ref)
    swap = first_ref[0] == 0
    out_ref[:, :HEAD_DIM] = jnp.where(swap, mine, other)
    out_ref[:, HEAD_DIM:] = jnp.where(swap, other, mine)


def spatial(position, hidden, own, other):
    rows = hidden.shape[0]
    vmem = pl.BlockSpec(memory_space=pltpu.VMEM)
    return pl.pallas_call(
        spatial_kernel,
        out_shape=jax.ShapeDtypeStruct((rows, 2 * HEAD_DIM), BF16),
        in_specs=[pl.BlockSpec(memory_space=pltpu.SMEM), vmem, vmem, vmem],
        out_specs=vmem,
        compiler_params=pltpu.CompilerParams(vmem_limit_bytes=48 * MIB),
        name="spatial",
    )(position, hidden, own, other)


def out_kernel(part_ref, w_ref, state_ref, gain_ref, x_ref, h_ref):
    step = pl.program_id(0)
    width = w_ref.shape[2]
    depth = part_ref.shape[2]
    total = jnp.zeros((part_ref.shape[1], width), F32)
    for z in range(part_ref.shape[0]):
        total += dot(part_ref[z], w_ref[0, z * depth : (z + 1) * depth])
    columns = pl.ds(pl.multiple_of(step * width, width), width)
    x_ref[:, columns] = state_ref[:, columns].astype(F32) + total

    @pl.when(step == pl.num_programs(0) - 1)
    def _():
        h_ref[...] = normed(x_ref[...], gain_ref[...]).astype(BF16)


def out_project(parts, weight, state, gain):
    blocks, rows, depth = parts.shape
    columns, inputs, width = weight.shape
    model = columns * width
    return pl.pallas_call(
        out_kernel,
        grid=(columns,),
        out_shape=(
            jax.ShapeDtypeStruct((rows, model), F32),
            jax.ShapeDtypeStruct((rows, model), BF16),
        ),
        in_specs=[
            pl.BlockSpec((blocks, rows, depth), lambda c: (0, 0, 0)),
            pl.BlockSpec((1, inputs, width), lambda c: (c, 0, 0)),
            pl.BlockSpec((rows, model), lambda c: (0, 0)),
            pl.BlockSpec((1, model), lambda c: (0, 0)),
        ],
        out_specs=(
            pl.BlockSpec((rows, model), lambda c: (0, 0)),
            pl.BlockSpec((rows, model), lambda c: (0, 0)),
        ),
        compiler_params=pltpu.CompilerParams(vmem_limit_bytes=32 * MIB),
        name="out_project",
    )(parts, weight, state, gain)


def temporal_kernel(qkv_ref, seen_ref, out_ref):
    seen = seen_ref[...] > 0
    for head in range(2):
        pick = lambda kind: qkv_ref[
            :, (2 * kind + head) * HEAD_DIM : (2 * kind + head + 1) * HEAD_DIM
        ]
        query, keys, values = pick(0), pick(1), pick(2)
        scores = jnp.where(seen, dot_t(query, keys) * SCALE, -1e30)
        top = jnp.max(scores, axis=-1, keepdims=True)
        probs = jnp.exp(scores - top)
        total = jnp.sum(probs, axis=-1, keepdims=True)
        coarse = probs.astype(BF16)
        fine = (probs - coarse.astype(F32)).astype(BF16)
        result = (dot(coarse, values) + dot(fine, values)) / total
        out_ref[:, head * HEAD_DIM : (head + 1) * HEAD_DIM] = result.astype(BF16)


def temporal(qkv, seen):
    vmem = pl.BlockSpec(memory_space=pltpu.VMEM)
    return pl.pallas_call(
        temporal_kernel,
        out_shape=jax.ShapeDtypeStruct((qkv.shape[0], 2 * HEAD_DIM), BF16),
        in_specs=[vmem, vmem],
        out_specs=vmem,
        compiler_params=pltpu.CompilerParams(vmem_limit_bytes=48 * MIB),
        name="temporal",
    )(qkv, seen)


def project_kernel(first_ref, h_ref, own_ref, other_ref, out_ref):
    swap = first_ref[0] == 0
    hidden = h_ref[...]
    for kind in range(3):
        mine = dot(hidden, own_ref[kind]).astype(BF16)
        other = dot(hidden, other_ref[kind]).astype(BF16)
        start = 2 * kind * HEAD_DIM
        out_ref[:, start : start + HEAD_DIM] = jnp.where(swap, mine, other)
        out_ref[:, start + HEAD_DIM : start + 2 * HEAD_DIM] = jnp.where(swap, other, mine)


def project(position, hidden, own, other):
    vmem = pl.BlockSpec(memory_space=pltpu.VMEM)
    return pl.pallas_call(
        project_kernel,
        out_shape=jax.ShapeDtypeStruct((hidden.shape[0], 6 * HEAD_DIM), BF16),
        in_specs=[pl.BlockSpec(memory_space=pltpu.SMEM), vmem, vmem, vmem],
        out_specs=vmem,
        compiler_params=pltpu.CompilerParams(vmem_limit_bytes=32 * MIB),
        name="project",
    )(position, hidden, own, other)


def mlp_kernel(h_ref, in_ref, in2_ref, out_ref, out2_ref, o_ref):
    @pl.loop(0, h_ref.shape[0] // 256)
    def _(tile):
        rows = pl.ds(pl.multiple_of(tile * 256, 256), 256)
        hidden = h_ref[rows]
        total = None
        for w_in, w_out in ((in_ref, out_ref), (in2_ref, out2_ref)):
            inner = jax.nn.gelu(dot(hidden, w_in[...]), approximate=True).astype(BF16)
            term = dot(inner, w_out[...])
            total = term if total is None else total + term
        o_ref[rows] = total.astype(BF16)


def mlp(hidden, w_in, in_other, w_out, out_other):
    vmem = pl.BlockSpec(memory_space=pltpu.VMEM)
    return pl.pallas_call(
        mlp_kernel,
        out_shape=jax.ShapeDtypeStruct(hidden.shape, BF16),
        in_specs=[vmem] * 5,
        out_specs=vmem,
        compiler_params=pltpu.CompilerParams(vmem_limit_bytes=48 * MIB),
        name="mlp",
    )(hidden, w_in, in_other, w_out, out_other)


def body(
    video, frame_ids, gains, spatial_qkv, spatial_out, temporal_qkv, temporal_out, mlp_in, mlp_out
):
    xh = lax.axis_index("xh")
    model = video.shape[-1]
    first = xh == 0
    place = xh.astype(jnp.int32).reshape(1)

    def after(value, earlier):
        return lax.optimization_barrier((value, earlier))[0]

    def piece(weight):
        block = lax.axis_index("y") * 2 + lax.axis_index("c")
        width = model // 8
        own = lax.dynamic_slice_in_dim(weight, block * width, width, 1)
        other = lax.ppermute(own, "xh", SWAP)
        return jnp.concatenate(
            [jnp.where(first, own, other), jnp.where(first, other, own)], axis=0
        )

    def along_z(part):
        return lax.all_gather(part, "z", axis=0, tiled=True)

    def blocks(part):
        return lax.all_gather(part, ("y", "c"), axis=0)

    grouped = jnp.transpose(video.reshape(2, 8, 4, model), (0, 2, 1, 3))
    keep = lax.dynamic_slice_in_dim(grouped, 2 * xh, 2, 1)
    give = lax.dynamic_slice_in_dim(grouped, 2 * (1 - xh), 2, 1)
    got = lax.ppermute(give, "xh", SWAP)
    state = jnp.concatenate(
        [jnp.where(first, keep, got), jnp.where(first, got, keep)], axis=0
    ).reshape(64, model)

    hidden = normed(state.astype(F32), gains[0]).astype(BF16)
    spatial_part = along_z(piece(spatial_out))
    temporal_part = piece(after(temporal_out, spatial_part))
    spatial_other = lax.ppermute(after(spatial_qkv, got), "xh", SWAP)
    hidden, spatial_part = ring_gather(hidden, spatial_part)
    spatial_whole = blocks(spatial_part)
    temporal_other = lax.ppermute(after(temporal_qkv, spatial_other), "xh", SWAP)
    heads = spatial(place, hidden.reshape(512, model), spatial_qkv, spatial_other)
    parts = lax.all_to_all(heads.reshape(8, 64, 256), "z", 0, 0, tiled=True)
    second, hidden = out_project(parts, spatial_whole, state, gains[1:2])

    stamps = lax.dynamic_slice_in_dim(frame_ids, 2 * xh, 2, 0).astype(F32)
    stamps = jnp.broadcast_to(stamps[:, None, None], (2, 8, 128)).reshape(16, 128)
    stamps = lax.all_gather(after(stamps, hidden), PEERS, axis=0, tiled=True)
    temporal_part = along_z(after(temporal_part, hidden))
    hidden, (temporal_part, stamps) = ring_gather(hidden, (temporal_part, stamps))
    temporal_whole = blocks(temporal_part)
    stamps = stamps[:, :1]
    count = stamps.shape[0]
    token = jnp.arange(count, dtype=jnp.int32) % 8
    seen = (stamps.reshape(1, count) <= stamps) & (token[None, :] == token[:, None])

    packed = project(place, hidden.reshape(512, model), temporal_qkv, temporal_other)
    in_other = lax.ppermute(after(mlp_in, packed), "xh", SWAP)
    packed = lax.all_to_all(packed.reshape(32, 16, 768), PEERS, 0, 0, tiled=True)
    heads = temporal(packed.reshape(512, 768), seen.astype(F32))
    heads = lax.all_to_all(heads.reshape(32, 16, 256), PEERS, 0, 0, tiled=True)
    out_other = lax.ppermute(after(mlp_out, heads), "xh", SWAP)
    parts = lax.all_to_all(heads.reshape(8, 64, 256), "z", 0, 0, tiled=True)
    third, hidden = out_project(parts, temporal_whole, second, gains[2:3])

    hidden, _ = ring_gather(hidden)
    partial = mlp(hidden.reshape(512, model), mlp_in, in_other, mlp_out, out_other)
    parts = lax.all_to_all(partial.reshape(8, 64, model), "z", 0, 0, tiled=True)
    result = (third + jnp.sum(parts.astype(F32), axis=0)).astype(BF16)

    result = result.reshape(2, 2, 2, 8, model)
    keep = lax.dynamic_index_in_dim(result, xh, 0, keepdims=False)
    give = lax.dynamic_index_in_dim(result, 1 - xh, 0, keepdims=False)
    got = lax.ppermute(give, "xh", SWAP)
    result = jnp.concatenate([jnp.where(first, keep, got), jnp.where(first, got, keep)], axis=1)
    return jnp.transpose(result, (0, 2, 1, 3)).reshape(16, 4, model)


def solution(mesh):
    fine = Mesh(mesh.devices.reshape(4, 2, 2, 8, 2), ("y", "xl", "c", "z", "xh"))
    space = ("z", "xh")
    return jax.shard_map(
        body,
        mesh=fine,
        in_specs=(
            P(space, TM, None),
            P(TM),
            P(),
            P(None, None, space),
            P(space, None),
            P(None, None, space),
            P(space, None),
            P(None, space),
            P(space, None),
        ),
        out_specs=P(space, TM, None),
        check_vma=False,
    )
```

time: 1060 us -> 472 us (0.45)
  waiting for transfers between devices: 970 us -> 242 us
  starting transfers between devices: 0.47 us -> 85.9 us
  blocking collectives: 10.5 us -> 74 us
  matrix products: 40.4 us -> 0 us
  Pallas kernels: 0 us -> 26.9 us
    reduce_scatter x3 -> x0, waiting for transfers between devices: 631 us -> none  [the longest x1 213 us: body(): lax.psum_scatter(jnp.einsum('pfd,de->pfe', rows, temporal_out, preferred_...]
    all_gather x4, waiting for transfers between devices: 339 us -> 9.13 us  [the longest x2 9.12 us: along_z(): return lax.all_gather(part, 'z', axis=0, tiled=True)]
    ppermute x0 -> x32, waiting for transfers between devices: none -> 161 us  [the longest x9 43.6 us: ring_gather(): fwd = lax.ppermute(fwd, 'z', right)]
    all_to_all x0 -> x4, waiting for transfers between devices: none -> 72 us  [the longest x1 49.1 us: body(): parts = lax.all_to_all(partial.reshape(8, 64, model), 'z', 0, 0, tiled=True)]
    all_gather x0 -> x1, blocking collectives: none -> 61.2 us  [body(): stamps = lax.all_gather(after(stamps, hidden), PEERS, axis=0, tiled=True)]
    ppermute x0 -> x32, starting transfers between devices: none -> 58.4 us  [the longest x9 29.7 us: ring_gather(): bwd = lax.ppermute(bwd, 'z', left)]
    dot_general x8 -> x0, matrix products: 39.9 us -> none  [the longest x2 9.99 us: project(): jnp.einsum('rfd,cde->rfce', piece, weight, preferred_element_type=jnp.flo...]
    all_to_all x0 -> x4, starting transfers between devices: none -> 27.4 us  [the longest x1 12.3 us: body(): lax.all_to_all(packed.reshape(32, 16, 768), PEERS, 0, 0, tiled=True)]
  transfers between devices with their start and end apart: 7 -> 40, of which waited for: 7 -> 25; matrix products, arithmetic and copies ran while one was open for 0% -> 2% of each run, Pallas kernels for 0% -> 3%
where the time goes in v1:
time: 472 us; the launch traced here: 463 us
  waiting for transfers between devices  242 us (51%)
  starting transfers between devices  85.9 us (18%)
  blocking collectives  74 us (16%)
  Pallas kernels  26.9 us (6%)
  local copies, waits for them, and re-layouts  16 us (3%)
  between operations  14.1 us (3%)
    all_gather x1, blocking collectives, body(): stamps = lax.all_gather(after(stamps, hidden), PEERS, axis=0, tiled=True)  61.2 us
    all_to_all x1, waiting for transfers between devices, body(): parts = lax.all_to_all(partial.reshape(8, 64, model), 'z', 0, 0, tiled=True)  49.1 us
    ppermute x9, waiting for transfers between devices, ring_gather(): fwd = lax.ppermute(fwd, 'z', right)  43.6 us
    ppermute x1, waiting for transfers between devices, body(): out_other = lax.ppermute(after(mlp_out, heads), 'xh', SWAP)  43 us
    ppermute x9, starting transfers between devices, ring_gather(): bwd = lax.ppermute(bwd, 'z', left)  29.7 us
    ppermute x1, waiting for transfers between devices, body(): lax.ppermute(after(temporal_qkv, spatial_other), 'xh', SWAP)  27.4 us
    ppermute x1, waiting for transfers between devices, body(): spatial_other = lax.ppermute(after(spatial_qkv, got), 'xh', SWAP)  23.3 us
    all_to_all x1, waiting for transfers between devices, body(): lax.all_to_all(packed.reshape(32, 16, 768), PEERS, 0, 0, tiled=True)  12.9 us
  transfers between devices with their start and end apart: 40, of which 25 were waited for; matrix products, arithmetic and copies ran while one was open for 2% of the time, Pallas kernels for 3%

profile of v1, /device:TPU:8, one launch (start us, length us, event | category | flops | bytes accessed | tf_op | source)
XLA Modules:
  0.0 463.3 jit_solution(6895567912098818932)
XLA Ops:
  6.5 1.3 constant_dynamic-slice_fusion.3
  7.9 3.1 collective-permute-start
  12.4 0.9 fusion.5
  13.3 4.3 collective-permute-done.7
  17.6 0.9 broadcast_select_fusion.5
  19.7 2.0 collective-permute-start.1
  21.7 4.0 collective-permute-start.2
  25.8 4.8 %collective-permute-done.1 = bf16[64,2048]{1,0:T(8,128)(2,1)S(1)} collective-permute-done((bf16[64,2048]{1,0:T(8,128)(2,1)S(1)}, bf16[64,2048]{1,0:T(8,128)(2,1)S(1)}, u32[]{:S(2)}, u32[]{:S(2)}) %collective-permute-start.1) | collective-permute-done | bytes 262176 | tf_op jit(solution)/shard_map/ppermute | solution.py:46
  30.5 3.2 collective-permute-start.4
  33.8 7.8 %collective-permute-done.3 = bf16[64,2048]{1,0:T(8,128)(2,1)S(1)} collective-permute-done((bf16[64,2048]{1,0:T(8,128)(2,1)S(1)}, bf16[64,2048]{1,0:T(8,128)(2,1)S(1)}, u32[]{:S(2)}, u32[]{:S(2)}) %collective-permute-start.3) | collective-permute-done | bytes 262176 | tf_op jit(solution)/shard_map/ppermute | solution.py:46
  41.6 3.2 collective-permute-start.6
  44.8 6.6 %collective-permute-done.5 = bf16[64,2048]{1,0:T(8,128)(2,1)S(1)} collective-permute-done((bf16[64,2048]{1,0:T(8,128)(2,1)S(1)}, bf16[64,2048]{1,0:T(8,128)(2,1)S(1)}, u32[]{:S(2)}, u32[]{:S(2)}) %collective-permute-start.5) | collective-permute-done | bytes 262176 | tf_op jit(solution)/shard_map/ppermute | solution.py:46
  51.5 9.1 %all-gather.7.cloned.1.call-done = bf16[2048,256]{1,0:T(8,128)(2,1)} async-done(((bf16[256,256]{1,0:T(8,128)(2,1)}), bf16[2048,256]{1,0:T(8,128)(2,1)}) %all-gather.7.cloned.1.call-update) | async-done | bytes 1048592 | tf_op jit(solution)/shard_map/all_gather | solution.py:236
  60.7 2.6 collective-permute-start.10
  64.3 1.8 collective-permute-start.8
  66.2 1.8 collective-permute-start.9
  67.9 2.7 collective-permute-done.8
  71.4 23.3 %collective-permute-done.10.other_ref = bf16[3,2048,128]{2,1,0:T(8,128)(2,1)S(1)} collective-permute-done((bf16[3,2048,128]{2,1,0:T(8,128)(2,1)S(1)}, bf16[3,2048,128]{2,1,0:T(8,128)(2,1)S(1)}, u32[]{:S(2)}, u32[]{:S(2)}) %collective-permute-start.10) | collective-permute-done | bytes 1572896 | tf_op jit(solution)/shard_map/ppermute | solution.py:252
  94.7 5.9 %spatial.1 = bf16[512,256]{1,0:T(8,128)(2,1)} custom-call(s32[1]{0:T(128)} %bitcast.first_ref, bf16[512,2048]{1,0:T(8,128)(2,1)S(1)} %bitcast.90, bf16[3,2048,128]{2,1,0:T(8,128)(2,1)S(1)} %copy-done.2, bf16[3,2048,128]{2,1,0:T(8,128)(2,1)S(1)} %collective-permute-done.10.other_ref), custom_call_target="tpu_custom_call" | custom-call | tf_op jit(solution)/shard_map/spatial/pallas_call | solution.py:87
  100.6 4.4 all-to-all-start
  105.1 0.9 constant_dynamic-slice_fusion
  106.0 3.2 collective-permute-start.17
  109.2 2.5 collective-permute-done.17
  111.7 0.9 broadcast_select_fusion.3
  113.3 2.3 all-to-all-done.part_ref
  115.6 3.4 copy-done
  118.9 2.7 out_project.2
  122.0 3.1 collective-permute-start.12
  125.0 4.3 collective-permute-done.11
  129.4 3.4 collective-permute-start.14
  132.8 6.4 %collective-permute-done.13 = bf16[64,2048]{1,0:T(8,128)(2,1)} collective-permute-done((bf16[64,2048]{1,0:T(8,128)(2,1)S(1)}, bf16[64,2048]{1,0:T(8,128)(2,1)}, u32[]{:S(2)}, u32[]{:S(2)}) %collective-permute-start.13) | collective-permute-done | bytes 262176 | tf_op jit(solution)/shard_map/ppermute | solution.py:46
  139.2 3.2 collective-permute-start.16
  142.8 61.2 %all_gather.25 = f32[512,128]{1,0:T(8,128)S(1)} all-gather(f32[16,128]{1,0:T(8,128)S(1)} %broadcast_in_dim.109), channel_id=1, replica_groups=mesh['y'=4,'xl'=2,'c'=2,'z'=8,'xh'=2] {'y','xl','c','xh'}, dimensions={0}, use_global_device_ids=true | all-gather | bytes 270336 | tf_op jit(solution)/shard_map/all_gather | solution.py:262
  205.1 1.0 bitcast_dynamic-update-slice_fusion.10
  206.1 1.0 bitcast_dynamic-update-slice_fusion.9
  207.3 3.5 collective-permute-start.19
  210.8 2.6 collective-permute-done.18
  213.4 27.4 %collective-permute-done.20.other_ref = bf16[3,2048,128]{2,1,0:T(8,128)(2,1)S(1)} collective-permute-done((bf16[3,2048,128]{2,1,0:T(8,128)(2,1)S(1)}, bf16[3,2048,128]{2,1,0:T(8,128)(2,1)S(1)}, u32[]{:S(2)}, u32[]{:S(2)}) %collective-permute-start.20) | collective-permute-done | bytes 1572896 | tf_op jit(solution)/shard_map/ppermute | solution.py:255
  240.8 4.3 project.1
  245.1 12.3 %all-to-all-start.1 = ((bf16[32,16,768]{2,1,0:T(8,128)(2,1)}), bf16[32,16,768]{2,1,0:T(8,128)(2,1)S(1)}, u32[]{:S(2)}, u32[]{:S(2)}) async-start(bf16[32,16,768]{2,1,0:T(8,128)(2,1)} %bitcast.28), calls=%async_computation.1 | async-start | bytes 1572864 | tf_op jit(solution)/shard_map/all_to_all | solution.py:273
  257.9 12.9 %all-to-all-done.1 = bf16[32,16,768]{2,1,0:T(8,128)(2,1)S(1)} async-done(((bf16[32,16,768]{2,1,0:T(8,128)(2,1)}), bf16[32,16,768]{2,1,0:T(8,128)(2,1)S(1)}, u32[]{:S(2)}, u32[]{:S(2)}) %all-to-all-start.1) | async-done | bytes 786464 | tf_op jit(solution)/shard_map/all_to_all | solution.py:273
  270.8 1.4 temporal.1
  272.2 12.8 %all_to_all.25 = bf16[32,16,256]{2,1,0:T(8,128)(2,1)} all-to-all(bf16[32,16,256]{2,1,0:T(8,128)(2,1)S(1)} %bitcast.94), channel_id=1, replica_groups=mesh['y'=4,'xl'=2,'c'=2,'z'=8,'xh'=2] {'y','xl','c','xh'}, dimensions={0} | all-to-all | bytes 524288 | tf_op jit(solution)/shard_map/all_to_all | solution.py:275
  285.0 3.7 all-to-all-start.3
  289.6 2.7 collective-permute-start.30
  292.3 7.7 %all-to-all-done.3.part_ref = bf16[8,64,256]{2,1,0:T(8,128)(2,1)S(1)} async-done(((bf16[8,64,256]{2,1,0:T(8,128)(2,1)}), bf16[8,64,256]{2,1,0:T(8,128)(2,1)S(1)}, u32[]{:S(2)}, u32[]{:S(2)}) %all-to-all-start.3) | async-done | bytes 262176 | tf_op jit(solution)/shard_map/all_to_all | solution.py:277
  300.0 3.4 copy-done.1
  303.4 2.7 out_project.3
  306.7 2.7 collective-permute-start.22
  309.7 4.1 collective-permute-done.21
  313.8 3.3 collective-permute-start.24
  317.1 4.6 collective-permute-done.23
  321.7 3.6 collective-permute-start.26
  325.3 5.0 %collective-permute-done.25 = bf16[64,2048]{1,0:T(8,128)(2,1)S(1)} collective-permute-done((bf16[64,2048]{1,0:T(8,128)(2,1)S(1)}, bf16[64,2048]{1,0:T(8,128)(2,1)S(1)}, u32[]{:S(2)}, u32[]{:S(2)}) %collective-permute-start.25) | collective-permute-done | bytes 262176 | tf_op jit(solution)/shard_map/ppermute | solution.py:46
  330.5 3.9 collective-permute-start.28
  334.4 2.2 collective-permute-done.27
  336.9 2.2 collective-permute-done.29.in2_ref
  339.0 43.0 %collective-permute-done.30.out2_ref = bf16[512,2048]{1,0:T(8,128)(2,1)} collective-permute-done((bf16[512,2048]{1,0:T(8,128)(2,1)}, bf16[512,2048]{1,0:T(8,128)(2,1)}, u32[]{:S(2)}, u32[]{:S(2)}) %collective-permute-start.30) | collective-permute-done | bytes 2097184 | tf_op jit(solution)/shard_map/ppermute | solution.py:276
  382.0 9.9 %mlp.1 = bf16[512,2048]{1,0:T(8,128)(2,1)} custom-call(bf16[512,2048]{1,0:T(8,128)(2,1)S(1)} %bitcast.91, bf16[2048,512]{1,0:T(8,128)(2,1)} %in_ref.1, bf16[2048,512]{1,0:T(8,128)(2,1)} %copy-done.4, bf16[512,2048]{1,0:T(8,128)(2,1)} %out_ref.1, bf16[512,2048]{1,0:T(8,128)(2,1)} %collective-permute-done.30.out2_ref), custom_call_target="tpu_custom_call" | custom-call | tf_op jit(solution)/shard_map/mlp/pallas_call | solution.py:205
  392.0 6.9 %all-to-all-start.4 = ((bf16[8,64,2048]{2,1,0:T(8,128)(2,1)}), bf16[8,64,2048]{2,1,0:T(8,128)(2,1)S(1)}, u32[]{:S(2)}, u32[]{:S(2)}) async-start(bf16[8,64,2048]{2,1,0:T(8,128)(2,1)} %bitcast.43), calls=%async_computation.4 | async-start | bytes 4194304 | tf_op jit(solution)/shard_map/all_to_all | solution.py:282
  398.8 49.1 %all-to-all-done.4 = bf16[8,64,2048]{2,1,0:T(8,128)(2,1)S(1)} async-done(((bf16[8,64,2048]{2,1,0:T(8,128)(2,1)}), bf16[8,64,2048]{2,1,0:T(8,128)(2,1)S(1)}, u32[]{:S(2)}, u32[]{:S(2)}) %all-to-all-start.4) | async-done | bytes 2097184 | tf_op jit(solution)/shard_map/all_to_all | solution.py:282
  448.3 1.0 collective-permute-start.31
  449.4 5.9 %collective-permute-done.31 = bf16[2,2,8,2048]{3,2,1,0:T(8,128)(2,1)S(1)} collective-permute-done((bf16[2,2,8,2048]{3,2,1,0:T(8,128)(2,1)S(1)}, bf16[2,2,8,2048]{3,2,1,0:T(8,128)(2,1)S(1)}, u32[]{:S(2)}, u32[]{:S(2)}) %collective-permute-start.31) | collective-permute-done | bytes 131104 | tf_op jit(solution)/shard_map/ppermute | solution.py:288
  455.4 0.9 copy.18
  (120 shorter events, 10.1 us)
Async XLA Ops:
  6.5 54.0 %all-gather.7.cloned.1.call-start = ((), (), s32[]{:S(2)}) async-start(), calls=%async_computation.5 | async-start | bytes 1179648 | tf_op jit(solution)/shard_map/all_gather | solution.py:236
  7.9 11.3 %collective-permute-start = (bf16[2,2,8,2048]{3,2,1,0:T(8,128)(2,1)S(1)}, bf16[2,2,8,2048]{3,2,1,0:T(8,128)(2,1)S(1)}, u32[]{:S(2)}, u32[]{:S(2)}) collective-permute-start(bf16[2,2,8,2048]{3,2,1,0:T(8,128)(2,1)S(1)} %bitcast.99), channel_id=1, source_target_pairs={{0,1},{1,0},{2,3},{3,2},{4,5},{5,4},{6,7},{7,6},{8,9},{9,8},{10,11... | collective-permute-start | bytes 393224 | tf_op jit(solution)/shard_map/ppermute | solution.py:244
  11.9 5.8 %collective-permute-start.7 = (bf16[128,256]{1,0:T(8,128)(2,1)S(1)}, bf16[128,256]{1,0:T(8,128)(2,1)S(1)}, u32[]{:S(2)}, u32[]{:S(2)}) collective-permute-start(bf16[128,256]{1,0:T(8,128)(2,1)S(1)} %constant_dynamic-slice_fusion.1), channel_id=1, source_target_pairs={{0,1},{1,0},{2,3},{3,2},{4,5},{5,4},{6,7},{7,6},{8,9},{9,8},{10,11... | collective-permute-start | bytes 196616 | tf_op jit(solution)/shard_map/ppermute | solution.py:230
  13.3 47.4 %copy-start.2 = (bf16[3,2048,128]{2,1,0:T(8,128)(2,1)S(1)}, bf16[3,2048,128]{2,1,0:T(8,128)(2,1)}, u32[]{:S(2)}) copy-start(bf16[3,2048,128]{2,1,0:T(8,128)(2,1)} %own_ref.2) | copy-start | bytes 4718596
  19.2 96.4 %all-gather.11.cloned.1.call-start = ((), (), s32[]{:S(2)}) async-start(), calls=%async_computation.7 | async-start | bytes 9437184 | tf_op jit(solution)/shard_map/all_gather | solution.py:239
  19.7 10.8 %collective-permute-start.1 = (bf16[64,2048]{1,0:T(8,128)(2,1)S(1)}, bf16[64,2048]{1,0:T(8,128)(2,1)S(1)}, u32[]{:S(2)}, u32[]{:S(2)}) collective-permute-start(bf16[64,2048]{1,0:T(8,128)(2,1)S(1)} %multiply_convert_fusion), channel_id=1, source_target_pairs={{0,2},{2,4},{4,6},{6,8},{8,10},{10,12},{12,14},{14,0},{1,3},{3,5},... | collective-permute-start | bytes 786440 | tf_op jit(solution)/shard_map/ppermute | solution.py:46
  21.7 8.8 %collective-permute-start.2 = (bf16[64,2048]{1,0:T(8,128)(2,1)S(1)}, bf16[64,2048]{1,0:T(8,128)(2,1)S(1)}, u32[]{:S(2)}, u32[]{:S(2)}) collective-permute-start(bf16[64,2048]{1,0:T(8,128)(2,1)S(1)} %multiply_convert_fusion), channel_id=1, source_target_pairs={{0,14},{2,0},{4,2},{6,4},{8,6},{10,8},{12,10},{14,12},{1,15},{3,1}... | collective-permute-start | bytes 786440 | tf_op jit(solution)/shard_map/ppermute | solution.py:47
  30.5 11.0 %collective-permute-start.3 = (bf16[64,2048]{1,0:T(8,128)(2,1)S(1)}, bf16[64,2048]{1,0:T(8,128)(2,1)S(1)}, u32[]{:S(2)}, u32[]{:S(2)}) collective-permute-start(bf16[64,2048]{1,0:T(8,128)(2,1)S(1)} %collective-permute-done.1), channel_id=1, source_target_pairs={{0,2},{2,4},{4,6},{6,8},{8,10},{10,12},{12,14},{14,0},{1,3},{3,5},... | collective-permute-start | bytes 786440 | tf_op jit(solution)/shard_map/ppermute | solution.py:46
  30.5 11.0 %collective-permute-start.4 = (bf16[64,2048]{1,0:T(8,128)(2,1)S(1)}, bf16[64,2048]{1,0:T(8,128)(2,1)S(1)}, u32[]{:S(2)}, u32[]{:S(2)}) collective-permute-start(bf16[64,2048]{1,0:T(8,128)(2,1)S(1)} %collective-permute-done.2), channel_id=1, source_target_pairs={{0,14},{2,0},{4,2},{6,4},{8,6},{10,8},{12,10},{14,12},{1,15},{3,1}... | collective-permute-start | bytes 786440 | tf_op jit(solution)/shard_map/ppermute | solution.py:47
  41.6 9.9 %copy-start.5 = (bf16[64,2048]{1,0:T(8,128)(2,1)}, bf16[64,2048]{1,0:T(8,128)(2,1)S(1)}, u32[]{:S(2)}) copy-start(bf16[64,2048]{1,0:T(8,128)(2,1)S(1)} %collective-permute-done.3) | copy-start | bytes 786436
  41.6 9.9 %collective-permute-start.5 = (bf16[64,2048]{1,0:T(8,128)(2,1)S(1)}, bf16[64,2048]{1,0:T(8,128)(2,1)S(1)}, u32[]{:S(2)}, u32[]{:S(2)}) collective-permute-start(bf16[64,2048]{1,0:T(8,128)(2,1)S(1)} %collective-permute-done.3), channel_id=1, source_target_pairs={{0,2},{2,4},{4,6},{6,8},{8,10},{10,12},{12,14},{14,0},{1,3},{3,5},... | collective-permute-start | bytes 786440 | tf_op jit(solution)/shard_map/ppermute | solution.py:46
  41.6 9.9 %copy-start.7 = (bf16[64,2048]{1,0:T(8,128)(2,1)}, bf16[64,2048]{1,0:T(8,128)(2,1)S(1)}, u32[]{:S(2)}) copy-start(bf16[64,2048]{1,0:T(8,128)(2,1)S(1)} %collective-permute-done.4) | copy-start | bytes 786436
  41.6 9.9 %collective-permute-start.6 = (bf16[64,2048]{1,0:T(8,128)(2,1)S(1)}, bf16[64,2048]{1,0:T(8,128)(2,1)S(1)}, u32[]{:S(2)}, u32[]{:S(2)}) collective-permute-start(bf16[64,2048]{1,0:T(8,128)(2,1)S(1)} %collective-permute-done.4), channel_id=1, source_target_pairs={{0,14},{2,0},{4,2},{6,4},{8,6},{10,8},{12,10},{14,12},{1,15},{3,1}... | collective-permute-start | bytes 786440 | tf_op jit(solution)/shard_map/ppermute | solution.py:47
  60.7 3.1 copy-start.6
  60.7 34.0 %collective-permute-start.10 = (bf16[3,2048,128]{2,1,0:T(8,128)(2,1)S(1)}, bf16[3,2048,128]{2,1,0:T(8,128)(2,1)S(1)}, u32[]{:S(2)}, u32[]{:S(2)}) collective-permute-start(bf16[3,2048,128]{2,1,0:T(8,128)(2,1)S(1)} %copy-done.2), channel_id=1, source_target_pairs={{0,1},{1,0},{2,3},{3,2},{4,5},{5,4},{6,7},{7,6},{8,9},{9,8},{10,11... | collective-permute-start | bytes 4718600 | tf_op jit(solution)/shard_map/ppermute | solution.py:252
  63.3 0.9 copy-start.8
  64.3 6.3 %collective-permute-start.8 = (bf16[32,2048]{1,0:T(8,128)(2,1)S(1)}, bf16[32,2048]{1,0:T(8,128)(2,1)S(1)}, u32[]{:S(2)}, u32[]{:S(2)}) collective-permute-start(bf16[32,2048]{1,0:T(8,128)(2,1)S(1)} %slice.31), channel_id=1, source_target_pairs={{0,2},{2,4},{4,6},{6,8},{8,10},{10,12},{12,14},{14,0},{1,3},{3,5},... | collective-permute-start | bytes 393224 | tf_op jit(solution)/shard_map/ppermute | solution.py:53
  66.2 5.2 %collective-permute-start.9 = (bf16[32,2048]{1,0:T(8,128)(2,1)S(1)}, bf16[32,2048]{1,0:T(8,128)(2,1)S(1)}, u32[]{:S(2)}, u32[]{:S(2)}) collective-permute-start(bf16[32,2048]{1,0:T(8,128)(2,1)S(1)} %slice.32), channel_id=1, source_target_pairs={{0,14},{2,0},{4,2},{6,4},{8,6},{10,8},{12,10},{14,12},{1,15},{3,1}... | collective-permute-start | bytes 393224 | tf_op jit(solution)/shard_map/ppermute | solution.py:54
  100.6 14.9 %all-to-all-start = ((bf16[8,64,256]{2,1,0:T(8,128)(2,1)}), bf16[8,64,256]{2,1,0:T(8,128)(2,1)S(1)}, u32[]{:S(2)}, u32[]{:S(2)}) async-start(bf16[8,64,256]{2,1,0:T(8,128)(2,1)} %bitcast.16), calls=%async_computation | async-start | bytes 524288 | tf_op jit(solution)/shard_map/all_to_all | solution.py:257
  105.1 98.9 %all-gather.9.cloned.1.call-start = ((), (), s32[]{:S(2)}) async-start(), calls=%async_computation.6 | async-start | bytes 1179648 | tf_op jit(solution)/shard_map/all_gather | solution.py:236
  106.0 5.8 %collective-permute-start.17 = (bf16[128,256]{1,0:T(8,128)(2,1)S(1)}, bf16[128,256]{1,0:T(8,128)(2,1)S(1)}, u32[]{:S(2)}, u32[]{:S(2)}) collective-permute-start(bf16[128,256]{1,0:T(8,128)(2,1)S(1)} %constant_dynamic-slice_fusion), channel_id=1, source_target_pairs={{0,1},{1,0},{2,3},{3,2},{4,5},{5,4},{6,7},{7,6},{8,9},{9,8},{10,11... | collective-permute-start | bytes 196616 | tf_op jit(solution)/shard_map/ppermute | solution.py:230
  115.6 3.4 copy-start
  118.9 23.5 %copy-start.13 = (s32[4]{0:T(128)S(1)}, s32[4]{0:T(128)}, u32[]{:S(2)}) copy-start(s32[4]{0:T(128)} %param.10) | copy-start | bytes 52
  118.9 85.1 %copy-start.3 = (bf16[3,2048,128]{2,1,0:T(8,128)(2,1)S(1)}, bf16[3,2048,128]{2,1,0:T(8,128)(2,1)}, u32[]{:S(2)}) copy-start(bf16[3,2048,128]{2,1,0:T(8,128)(2,1)} %own_ref.3) | copy-start | bytes 4718596
  121.7 178.3 %all-gather.13.cloned.1.call-start = ((), (), s32[]{:S(2)}) async-start(), calls=%async_computation.8 | async-start | bytes 9437184 | tf_op jit(solution)/shard_map/all_gather | solution.py:239
  121.7 7.7 %collective-permute-start.11 = (bf16[64,2048]{1,0:T(8,128)(2,1)S(1)}, bf16[64,2048]{1,0:T(8,128)(2,1)S(1)}, u32[]{:S(2)}, u32[]{:S(2)}) collective-permute-start(bf16[64,2048]{1,0:T(8,128)(2,1)S(1)} %get-tuple-element.27), channel_id=1, source_target_pairs={{0,2},{2,4},{4,6},{6,8},{8,10},{10,12},{12,14},{14,0},{1,3},{3,5},... | collective-permute-start | bytes 786440 | tf_op jit(solution)/shard_map/ppermute | solution.py:46
  122.0 7.4 %collective-permute-start.12 = (bf16[64,2048]{1,0:T(8,128)(2,1)S(1)}, bf16[64,2048]{1,0:T(8,128)(2,1)S(1)}, u32[]{:S(2)}, u32[]{:S(2)}) collective-permute-start(bf16[64,2048]{1,0:T(8,128)(2,1)S(1)} %get-tuple-element.27), channel_id=1, source_target_pairs={{0,14},{2,0},{4,2},{6,4},{8,6},{10,8},{12,10},{14,12},{1,15},{3,1}... | collective-permute-start | bytes 786440 | tf_op jit(solution)/shard_map/ppermute | solution.py:47
  129.4 9.8 %copy-start.9 = (bf16[64,2048]{1,0:T(8,128)(2,1)}, bf16[64,2048]{1,0:T(8,128)(2,1)S(1)}, u32[]{:S(2)}) copy-start(bf16[64,2048]{1,0:T(8,128)(2,1)S(1)} %collective-permute-done.11) | copy-start | bytes 786436
  129.4 9.8 %collective-permute-start.13 = (bf16[64,2048]{1,0:T(8,128)(2,1)S(1)}, bf16[64,2048]{1,0:T(8,128)(2,1)}, u32[]{:S(2)}, u32[]{:S(2)}) collective-permute-start(bf16[64,2048]{1,0:T(8,128)(2,1)S(1)} %collective-permute-done.11), channel_id=1, source_target_pairs={{0,2},{2,4},{4,6},{6,8},{8,10},{10,12},{12,14},{14,0},{1,3},{3,5},... | collective-permute-start | bytes 786440 | tf_op jit(solution)/shard_map/ppermute | solution.py:46
  129.4 13.3 %copy-start.11 = (bf16[64,2048]{1,0:T(8,128)(2,1)}, bf16[64,2048]{1,0:T(8,128)(2,1)S(1)}, u32[]{:S(2)}) copy-start(bf16[64,2048]{1,0:T(8,128)(2,1)S(1)} %collective-permute-done.12) | copy-start | bytes 786436
  129.4 9.8 %collective-permute-start.14 = (bf16[64,2048]{1,0:T(8,128)(2,1)S(1)}, bf16[64,2048]{1,0:T(8,128)(2,1)}, u32[]{:S(2)}, u32[]{:S(2)}) collective-permute-start(bf16[64,2048]{1,0:T(8,128)(2,1)S(1)} %collective-permute-done.12), channel_id=1, source_target_pairs={{0,14},{2,0},{4,2},{6,4},{8,6},{10,8},{12,10},{14,12},{1,15},{3,1}... | collective-permute-start | bytes 786440 | tf_op jit(solution)/shard_map/ppermute | solution.py:47
  139.2 64.8 %collective-permute-start.15 = (bf16[64,2048]{1,0:T(8,128)(2,1)}, bf16[64,2048]{1,0:T(8,128)(2,1)S(1)}, u32[]{:S(2)}, u32[]{:S(2)}) collective-permute-start(bf16[64,2048]{1,0:T(8,128)(2,1)} %collective-permute-done.13), channel_id=1, source_target_pairs={{0,2},{2,4},{4,6},{6,8},{8,10},{10,12},{12,14},{14,0},{1,3},{3,5},... | collective-permute-start | bytes 786440 | tf_op jit(solution)/shard_map/ppermute | solution.py:46
  139.2 64.8 %collective-permute-start.16 = (bf16[64,2048]{1,0:T(8,128)(2,1)}, bf16[64,2048]{1,0:T(8,128)(2,1)S(1)}, u32[]{:S(2)}, u32[]{:S(2)}) collective-permute-start(bf16[64,2048]{1,0:T(8,128)(2,1)} %collective-permute-done.14), channel_id=1, source_target_pairs={{0,14},{2,0},{4,2},{6,4},{8,6},{10,8},{12,10},{14,12},{1,15},{3,1}... | collective-permute-start | bytes 786440 | tf_op jit(solution)/shard_map/ppermute | solution.py:47
  204.0 1.0 copy-start.10
  204.1 1.0 copy-start.12
  204.1 36.8 %collective-permute-start.20 = (bf16[3,2048,128]{2,1,0:T(8,128)(2,1)S(1)}, bf16[3,2048,128]{2,1,0:T(8,128)(2,1)S(1)}, u32[]{:S(2)}, u32[]{:S(2)}) collective-permute-start(bf16[3,2048,128]{2,1,0:T(8,128)(2,1)S(1)} %copy-done.3), channel_id=1, source_target_pairs={{0,1},{1,0},{2,3},{3,2},{4,5},{5,4},{6,7},{7,6},{8,9},{9,8},{10,11... | collective-permute-start | bytes 4718600 | tf_op jit(solution)/shard_map/ppermute | solution.py:255
  207.1 6.3 %collective-permute-start.18 = (bf16[32,2048]{1,0:T(8,128)(2,1)S(1)}, bf16[32,2048]{1,0:T(8,128)(2,1)S(1)}, u32[]{:S(2)}, u32[]{:S(2)}) collective-permute-start(bf16[32,2048]{1,0:T(8,128)(2,1)S(1)} %slice.34), channel_id=1, source_target_pairs={{0,2},{2,4},{4,6},{6,8},{8,10},{10,12},{12,14},{14,0},{1,3},{3,5},... | collective-permute-start | bytes 393224 | tf_op jit(solution)/shard_map/ppermute | solution.py:53
  207.3 6.1 %collective-permute-start.19 = (bf16[32,2048]{1,0:T(8,128)(2,1)S(1)}, bf16[32,2048]{1,0:T(8,128)(2,1)S(1)}, u32[]{:S(2)}, u32[]{:S(2)}) collective-permute-start(bf16[32,2048]{1,0:T(8,128)(2,1)S(1)} %slice.35), channel_id=1, source_target_pairs={{0,14},{2,0},{4,2},{6,4},{8,6},{10,8},{12,10},{14,12},{1,15},{3,1}... | collective-permute-start | bytes 393224 | tf_op jit(solution)/shard_map/ppermute | solution.py:54
  245.1 25.7 %all-to-all-start.1 = ((bf16[32,16,768]{2,1,0:T(8,128)(2,1)}), bf16[32,16,768]{2,1,0:T(8,128)(2,1)S(1)}, u32[]{:S(2)}, u32[]{:S(2)}) async-start(bf16[32,16,768]{2,1,0:T(8,128)(2,1)} %bitcast.28), calls=%async_computation.1 | async-start | bytes 1572864 | tf_op jit(solution)/shard_map/all_to_all | solution.py:273
  285.0 15.0 %all-to-all-start.3 = ((bf16[8,64,256]{2,1,0:T(8,128)(2,1)}), bf16[8,64,256]{2,1,0:T(8,128)(2,1)S(1)}, u32[]{:S(2)}, u32[]{:S(2)}) async-start(bf16[8,64,256]{2,1,0:T(8,128)(2,1)} %bitcast.31), calls=%async_computation.3 | async-start | bytes 524288 | tf_op jit(solution)/shard_map/all_to_all | solution.py:277
  288.8 50.3 %collective-permute-start.29 = (bf16[2048,512]{1,0:T(8,128)(2,1)}, bf16[2048,512]{1,0:T(8,128)(2,1)S(1)}, u32[]{:S(2)}, u32[]{:S(2)}) collective-permute-start(bf16[2048,512]{1,0:T(8,128)(2,1)} %in_ref.1), channel_id=1, source_target_pairs={{0,1},{1,0},{2,3},{3,2},{4,5},{5,4},{6,7},{7,6},{8,9},{9,8},{10,11... | collective-permute-start | bytes 6291464 | tf_op jit(solution)/shard_map/ppermute | solution.py:272
  289.6 92.5 %collective-permute-start.30 = (bf16[512,2048]{1,0:T(8,128)(2,1)}, bf16[512,2048]{1,0:T(8,128)(2,1)}, u32[]{:S(2)}, u32[]{:S(2)}) collective-permute-start(bf16[512,2048]{1,0:T(8,128)(2,1)} %out_ref.1), channel_id=1, source_target_pairs={{0,1},{1,0},{2,3},{3,2},{4,5},{5,4},{6,7},{7,6},{8,9},{9,8},{10,11... | collective-permute-start | bytes 6291464 | tf_op jit(solution)/shard_map/ppermute | solution.py:276
  300.0 3.4 copy-start.1
  306.1 7.7 %collective-permute-start.21 = (bf16[64,2048]{1,0:T(8,128)(2,1)S(1)}, bf16[64,2048]{1,0:T(8,128)(2,1)S(1)}, u32[]{:S(2)}, u32[]{:S(2)}) collective-permute-start(bf16[64,2048]{1,0:T(8,128)(2,1)S(1)} %get-tuple-element.38), channel_id=1, source_target_pairs={{0,2},{2,4},{4,6},{6,8},{8,10},{10,12},{12,14},{14,0},{1,3},{3,5},... | collective-permute-start | bytes 786440 | tf_op jit(solution)/shard_map/ppermute | solution.py:46
  306.7 7.0 %collective-permute-start.22 = (bf16[64,2048]{1,0:T(8,128)(2,1)S(1)}, bf16[64,2048]{1,0:T(8,128)(2,1)S(1)}, u32[]{:S(2)}, u32[]{:S(2)}) collective-permute-start(bf16[64,2048]{1,0:T(8,128)(2,1)S(1)} %get-tuple-element.38), channel_id=1, source_target_pairs={{0,14},{2,0},{4,2},{6,4},{8,6},{10,8},{12,10},{14,12},{1,15},{3,1}... | collective-permute-start | bytes 786440 | tf_op jit(solution)/shard_map/ppermute | solution.py:47
  313.7 7.9 %collective-permute-start.23 = (bf16[64,2048]{1,0:T(8,128)(2,1)S(1)}, bf16[64,2048]{1,0:T(8,128)(2,1)S(1)}, u32[]{:S(2)}, u32[]{:S(2)}) collective-permute-start(bf16[64,2048]{1,0:T(8,128)(2,1)S(1)} %collective-permute-done.21), channel_id=1, source_target_pairs={{0,2},{2,4},{4,6},{6,8},{8,10},{10,12},{12,14},{14,0},{1,3},{3,5},... | collective-permute-start | bytes 786440 | tf_op jit(solution)/shard_map/ppermute | solution.py:46
  313.8 7.9 %collective-permute-start.24 = (bf16[64,2048]{1,0:T(8,128)(2,1)S(1)}, bf16[64,2048]{1,0:T(8,128)(2,1)S(1)}, u32[]{:S(2)}, u32[]{:S(2)}) collective-permute-start(bf16[64,2048]{1,0:T(8,128)(2,1)S(1)} %collective-permute-done.22), channel_id=1, source_target_pairs={{0,14},{2,0},{4,2},{6,4},{8,6},{10,8},{12,10},{14,12},{1,15},{3,1}... | collective-permute-start | bytes 786440 | tf_op jit(solution)/shard_map/ppermute | solution.py:47
  321.7 8.6 %collective-permute-start.25 = (bf16[64,2048]{1,0:T(8,128)(2,1)S(1)}, bf16[64,2048]{1,0:T(8,128)(2,1)S(1)}, u32[]{:S(2)}, u32[]{:S(2)}) collective-permute-start(bf16[64,2048]{1,0:T(8,128)(2,1)S(1)} %collective-permute-done.23), channel_id=1, source_target_pairs={{0,2},{2,4},{4,6},{6,8},{8,10},{10,12},{12,14},{14,0},{1,3},{3,5},... | collective-permute-start | bytes 786440 | tf_op jit(solution)/shard_map/ppermute | solution.py:46
  321.7 8.7 %collective-permute-start.26 = (bf16[64,2048]{1,0:T(8,128)(2,1)S(1)}, bf16[64,2048]{1,0:T(8,128)(2,1)S(1)}, u32[]{:S(2)}, u32[]{:S(2)}) collective-permute-start(bf16[64,2048]{1,0:T(8,128)(2,1)S(1)} %collective-permute-done.24), channel_id=1, source_target_pairs={{0,14},{2,0},{4,2},{6,4},{8,6},{10,8},{12,10},{14,12},{1,15},{3,1}... | collective-permute-start | bytes 786440 | tf_op jit(solution)/shard_map/ppermute | solution.py:47
  330.3 6.3 %collective-permute-start.27 = (bf16[32,2048]{1,0:T(8,128)(2,1)S(1)}, bf16[32,2048]{1,0:T(8,128)(2,1)S(1)}, u32[]{:S(2)}, u32[]{:S(2)}) collective-permute-start(bf16[32,2048]{1,0:T(8,128)(2,1)S(1)} %slice.40), channel_id=1, source_target_pairs={{0,2},{2,4},{4,6},{6,8},{8,10},{10,12},{12,14},{14,0},{1,3},{3,5},... | collective-permute-start | bytes 393224 | tf_op jit(solution)/shard_map/ppermute | solution.py:53
  330.5 6.4 %collective-permute-start.28 = (bf16[32,2048]{1,0:T(8,128)(2,1)S(1)}, bf16[32,2048]{1,0:T(8,128)(2,1)S(1)}, u32[]{:S(2)}, u32[]{:S(2)}) collective-permute-start(bf16[32,2048]{1,0:T(8,128)(2,1)S(1)} %slice.41), channel_id=1, source_target_pairs={{0,14},{2,0},{4,2},{6,4},{8,6},{10,8},{12,10},{14,12},{1,15},{3,1}... | collective-permute-start | bytes 393224 | tf_op jit(solution)/shard_map/ppermute | solution.py:54
  339.0 43.0 %copy-start.4 = (bf16[2048,512]{1,0:T(8,128)(2,1)}, bf16[2048,512]{1,0:T(8,128)(2,1)S(1)}, u32[]{:S(2)}) copy-start(bf16[2048,512]{1,0:T(8,128)(2,1)S(1)} %collective-permute-done.29.in2_ref) | copy-start | bytes 6291460
  392.0 55.9 %all-to-all-start.4 = ((bf16[8,64,2048]{2,1,0:T(8,128)(2,1)}), bf16[8,64,2048]{2,1,0:T(8,128)(2,1)S(1)}, u32[]{:S(2)}, u32[]{:S(2)}) async-start(bf16[8,64,2048]{2,1,0:T(8,128)(2,1)} %bitcast.43), calls=%async_computation.4 | async-start | bytes 4194304 | tf_op jit(solution)/shard_map/all_to_all | solution.py:282
  448.3 7.0 %collective-permute-start.31 = (bf16[2,2,8,2048]{3,2,1,0:T(8,128)(2,1)S(1)}, bf16[2,2,8,2048]{3,2,1,0:T(8,128)(2,1)S(1)}, u32[]{:S(2)}, u32[]{:S(2)}) collective-permute-start(bf16[2,2,8,2048]{3,2,1,0:T(8,128)(2,1)S(1)} %dynamic-slice_bitcast_fusion), channel_id=1, source_target_pairs={{0,1},{1,0},{2,3},{3,2},{4,5},{5,4},{6,7},{7,6},{8,9},{9,8},{10,11... | collective-permute-start | bytes 393224 | tf_op jit(solution)/shard_map/ppermute | solution.py:288
Sparse Core Ops, SparseCore 0:
  19.3 41.2 all-gather.6
  62.4 49.6 all-gather.10
  121.8 39.0 all-gather.8
  204.2 53.6 all-gather.12
